TPU v7x, 256 devices: a whole 4x4x8 slice. The times are simulated.
256 devices in a mesh: acq: 4 (over x), tile: 64 (over z, y, core).
Axes of the slice: x: 4, y: 4, z: 8, core: 2. Of those that a mesh axis runs over, the one named last changes fastest.
Arguments:
- slc: bfloat16 [16, 2, 8192, 1280], P('acq', None, 'tile')
- match: int32 [2, 16], replicated, may hold values from 0 to 3, as said below
- dest: int32 [64, 16, 32, 1], P('tile', 'acq'), may hold values from 0 to 3; in each aligned block of 128 rows (0 to 127, 128 to 255, ..., all dimensions but the last counted through in order) at most 64 rows name the same one
- coherent: int32 [64, 16, 32], P('tile', 'acq'), may hold values 0 or 1
Outputs:
- received: bfloat16 [64, 1024, 2, 128], P('tile', 'acq')
Inputs may be any that keep to these rules, and one draw needn't show every extreme that they name: `match`: within each round, the entries of each aligned run of 4 acquisitions are a permutation of 0 to 3. `dest`: among the 128 rows of one device, at most 64 name the same owner.
All inputs are finite; a program needn't handle non-finite values. No bound on the sum of `coherent` on one device may be relied on, other than what follows from the above.
Results may differ from a plain program's by a relative error of at most 0.001.
Values may be sent and summed in bfloat16 or wider, within the bound.
No kernel may reach another device: no remote copies, remote signals or barrier semaphores. Data moves between devices by JAX's collectives and lax.ppermute only.
A program may use at most 128 MiB of HBM per device.

v0:
```python
import jax
import jax.numpy as jnp
from jax import lax
from jax.sharding import PartitionSpec as P

PATCH = 32
LOOK_L = 4
LOOK_S = 20
BLOCK_ROWS = 4
ROUNDS = 2
power_floor = 0.25
energy_eps = 1e-06


def swapped(x, axis, stride):
    return lax.ppermute(x, axis, [(i, i ^ 1 << stride) for i in range(lax.axis_size(axis))])


def dft_tables():
    counter = jnp.arange(PATCH)
    phase = counter[:, None] * counter[None, :] % PATCH
    angle = phase.astype(jnp.float32) * (2.0 * 3.141592653589793 / PATCH)
    return (jnp.cos(angle), jnp.sin(angle))


def along_axes(real_part, imag_part, cosine, sine_tab, sign, form):
    hold = lax.Precision.HIGHEST
    c_real = jnp.einsum(form, cosine, real_part, precision=hold)
    c_imag = jnp.einsum(form, cosine, imag_part, precision=hold)
    s_real = jnp.einsum(form, sine_tab, real_part, precision=hold)
    s_imag = jnp.einsum(form, sine_tab, imag_part, precision=hold)
    return (c_real - sign * s_imag, c_imag + sign * s_real)


def transform(real_part, imag_part, cosine, sine_tab, sign):
    real_part, imag_part = along_axes(
        real_part, imag_part, cosine, sine_tab, sign, "jk,aPkQl->aPjQl"
    )
    return along_axes(real_part, imag_part, cosine, sine_tab, sign, "lm,aPkQm->aPkQl")


def cross_looks(left, right, picks):
    acq_dev, _, line_count, sample_count = left.shape
    other = jnp.take(right, picks, axis=0)
    own_real = left[:, 0].astype(jnp.float32)
    own_imag = left[:, 1].astype(jnp.float32)
    other_real = other[:, 0].astype(jnp.float32)
    other_imag = other[:, 1].astype(jnp.float32)
    real_part = own_real * other_real + own_imag * other_imag
    imag_part = own_imag * other_real - own_real * other_imag
    stacked = jnp.stack([real_part, imag_part], axis=1)
    stacked = stacked.reshape(
        acq_dev, 2, line_count // LOOK_L, LOOK_L, sample_count // LOOK_S, LOOK_S
    )
    return jnp.sum(stacked, axis=(3, 5)) / (LOOK_L * LOOK_S)


def shards(slc, match, dest, coherent):
    acq_dev, _, lines_dev, samples_dev = slc.shape
    n_acq = lax.axis_size("acq")
    n_tile = lax.axis_size("tile")
    far_bit = n_acq.bit_length() - 2
    grid_count = lines_dev * n_tile // LOOK_L * (samples_dev // LOOK_S)
    patch_rows = lines_dev // LOOK_L // PATCH
    patch_cols = samples_dev // LOOK_S // PATCH
    cosine, sine_tab = dft_tables()
    my_group = lax.axis_index("acq")

    def swap_tiles(tiles, round_number):
        if round_number == 0:
            return swapped(tiles, "acq", 0)
        return swapped(tiles, "acq", far_bit)

    order_list = [0, 1]
    looked_all = {}
    filtered_all = {}
    for round_number in order_list:
        own_match = lax.dynamic_slice_in_dim(match[round_number], my_group * acq_dev, acq_dev)
        group_tiles = swap_tiles(slc, round_number)
        looked_all[round_number] = cross_looks(slc, group_tiles, own_match)
        local_looked = looked_all[round_number]
        total = lax.psum(
            jnp.sum(local_looked[:, 0] ** 2 + local_looked[:, 1] ** 2, axis=(1, 2)), "tile"
        )
        energy = total / grid_count + energy_eps
        looked = looked_all[round_number]
        shape_six = (acq_dev, patch_rows, PATCH, patch_cols, PATCH)
        real_part = looked[:, 0].reshape(shape_six)
        imag_part = looked[:, 1].reshape(shape_six)
        spec_real, spec_imag = transform(real_part, imag_part, cosine, sine_tab, -1.0)
        scale = energy[:, None, None, None, None]
        power = (spec_real**2 + spec_imag**2) / (PATCH * PATCH * scale)
        weight = (power + power_floor) ** 0.25
        back_real, back_imag = transform(
            weight * spec_real, weight * spec_imag, cosine, sine_tab, 1.0
        )
        norm_factor = 1.0 / (PATCH * PATCH * jnp.sqrt(scale))
        parts = jnp.stack([back_real * norm_factor, back_imag * norm_factor], axis=-1)
        parts = parts.reshape(
            acq_dev, patch_rows, PATCH // BLOCK_ROWS, BLOCK_ROWS, patch_cols, PATCH, 2
        )
        parts = jnp.transpose(parts, (0, 1, 2, 4, 6, 3, 5))
        filtered_all[round_number] = parts.reshape(
            acq_dev, patch_rows * (PATCH // BLOCK_ROWS) * patch_cols, 2, BLOCK_ROWS * PATCH
        )
    stacked = jnp.stack([filtered_all[round_number] for round_number in range(ROUNDS)], axis=1)
    block_len = BLOCK_ROWS * PATCH
    rows_dev = stacked.shape[0] * stacked.shape[1] * stacked.shape[2]
    cap_rows = max(3, 2 * ((rows_dev + n_acq - 1) // n_acq))
    stacked = stacked.reshape(rows_dev, 2, block_len)
    mask_rows = coherent.reshape(rows_dev).astype(jnp.float32)
    value = (stacked * mask_rows[:, None, None]).astype(jnp.bfloat16)
    owner = dest.reshape(rows_dev)
    onehot = (owner[:, None] == jnp.arange(n_acq)).astype(jnp.int32)
    rank = jnp.sum((jnp.cumsum(onehot, axis=0) - onehot) * onehot, axis=1)
    hits = (onehot[:, :, None] == 1) & (rank[:, None, None] == jnp.arange(cap_rows)[None, None, :])
    select = hits.astype(jnp.bfloat16).reshape(rows_dev, n_acq * cap_rows)
    outgoing = jnp.einsum("ks,kcp->scp", select, value, preferred_element_type=jnp.float32).astype(
        jnp.bfloat16
    )
    incoming = lax.all_to_all(outgoing, "acq", split_axis=0, concat_axis=0, tiled=True)
    return incoming[None]


def solution(mesh):
    return jax.shard_map(
        shards,
        mesh=mesh,
        in_specs=(
            P("acq", None, "tile", None),
            P(),
            P("tile", "acq", None, None),
            P("tile", "acq", None),
        ),
        out_specs=P("tile", "acq", None, None),
        check_vma=False,
    )
```

profile of v0, /device:TPU:2, one launch (start us, length us, event | category | flops | bytes accessed | tf_op | source)
XLA Modules:
  0.0 392.0 jit_solution(11845834372850043596)
XLA Ops:
  0.0 2.1 collective-permute-start.1
  2.1 1.4 collective-permute-start
  3.6 0.7 convert_element_type.142
  4.3 0.5 broadcast.327
  4.8 1.3 reduce.5
  6.6 0.8 fusion.240
  7.8 53.8 %collective-permute-done.1 = bf16[4,2,128,1280]{3,2,1,0:T(8,128)(2,1)} collective-permute-done((bf16[4,2,128,1280]{3,2,1,0:T(8,128)(2,1)}, bf16[4,2,128,1280]{3,2,1,0:T(8,128)(2,1)}, u32[]{:S(2)}, u32[]{:S(2)}) %collective-permute-start.1) | collective-permute-done | bytes 2621472 | tf_op jit(solution)/shard_map/ppermute | solution.py:16
  61.6 2.5 gather_fusion.1
  64.0 1.8 broadcast_select_fusion
  65.9 50.8 %collective-permute-done = bf16[4,2,128,1280]{3,2,1,0:T(8,128)(2,1)} collective-permute-done((bf16[4,2,128,1280]{3,2,1,0:T(8,128)(2,1)}, bf16[4,2,128,1280]{3,2,1,0:T(8,128)(2,1)}, u32[]{:S(2)}, u32[]{:S(2)}) %collective-permute-start) | collective-permute-done | bytes 2621472 | tf_op jit(solution)/shard_map/ppermute | solution.py:16
  116.6 2.5 gather_fusion
  119.4 1.4 copy-done
  120.8 0.8 copy-done.1
  121.6 4.0 %fusion = (f32[4,1,128,1280]{3,2,1,0:T(8,128)}, f32[4,1,128,1280]{3,2,1,0:T(8,128)}, f32[4,1,128,1280]{3,2,1,0:T(8,128)S(1)}, f32[4,1,128,1280]{3,2,1,0:T(8,128)}) fusion(bf16[4,2,128,1280]{3,2,1,0:T(8,128)(2,1)S(1)} %broadcast_select_fusion.1, bf16[4,2,128,1280]{3,2,1,0:T(8,128)(2,1)S(1)} %copy-done.1, bf16[4,2,128,1280]{3,2,1,0:T(8,128)(2,1)S(1)} %copy-done), kind=kLoop, calls=%fused_computation.12 | loop fusion | flops 11796480 | bytes 18350080 | tf_op jit(solution)/shard_map/add | solution.py:49
  125.6 21.7 %stack.39 = f32[4,1,32,4,64,20]{5,4,3,2,0,1:T(8,128)} reshape(f32[4,1,128,1280]{3,2,1,0:T(8,128)} %get-tuple-element.12) | data formatting | bytes 5242880 | tf_op jit(solution)/shard_map/stack | solution.py:51
  147.3 21.7 %stack.40 = f32[4,1,32,4,64,20]{5,4,3,2,0,1:T(8,128)} reshape(f32[4,1,128,1280]{3,2,1,0:T(8,128)} %get-tuple-element.13) | data formatting | bytes 5242880 | tf_op jit(solution)/shard_map/stack | solution.py:51
  168.9 12.7 %maximum_reduce_fusion = f32[4,2,32,64]{3,2,0,1:T(8,128)S(1)} fusion(f32[4,1,32,4,64,20]{5,4,3,2,0,1:T(8,128)} %stack.40, f32[4,1,32,4,64,20]{5,4,3,2,0,1:T(8,128)} %stack.39), kind=kLoop, calls=%fused_computation.2 | loop fusion | flops 2605056 | bytes 5308416 | tf_op jit(solution)/shard_map/reduce_sum | solution.py:55
  185.0 21.7 %stack.45 = f32[4,1,32,4,64,20]{5,4,3,2,0,1:T(8,128)} reshape(f32[4,1,128,1280]{3,2,1,0:T(8,128)} %get-tuple-element.17) | data formatting | bytes 5242880 | tf_op jit(solution)/shard_map/stack | solution.py:51
  206.7 20.9 %stack.46 = f32[4,1,32,4,64,20]{5,4,3,2,0,1:T(8,128)} reshape(f32[4,1,128,1280]{3,2,1,0:T(8,128)S(1)} %get-tuple-element.16) | data formatting | bytes 5242880 | tf_op jit(solution)/shard_map/stack | solution.py:51
  227.6 12.7 %maximum_reduce_fusion.1 = f32[4,2,32,64]{3,2,0,1:T(8,128)S(1)} fusion(f32[4,1,32,4,64,20]{5,4,3,2,0,1:T(8,128)} %stack.46, f32[4,1,32,4,64,20]{5,4,3,2,0,1:T(8,128)} %stack.45), kind=kLoop, calls=%fused_computation.3 | loop fusion | flops 2605056 | bytes 5308416 | tf_op jit(solution)/shard_map/reduce_sum | solution.py:55
  240.5 131.1 %all-reduce = (f32[4]{0:T(128)S(1)}, f32[4]{0:T(128)S(1)}) all-reduce(f32[4]{0:T(128)S(1)} %get-tuple-element.21, f32[4]{0:T(128)S(1)} %get-tuple-element.19), channel_id=1, replica_groups=mesh['acq'=4,'tile'=64] {'tile'}, use_global_device_ids=true, to_apply=%region_7.9 | all-reduce | flops 8 | bytes 64 | tf_op jit(solution)/shard_map/psum | solution.py:82
  371.6 0.5 fusion.60
  372.1 0.5 fusion.56
  375.8 0.5 fusion.48
  376.3 0.5 fusion.44
  376.9 0.5 fusion.9
  377.8 0.5 fusion.8
  379.1 0.4 fusion.13
  379.8 0.5 fusion.5
  380.7 0.5 fusion.4
  383.1 8.2 %all_to_all.5 = bf16[256,2,128]{2,1,0:T(2,128)(2,1)S(1)} all-to-all(bf16[256,2,128]{2,1,0:T(2,128)(2,1)S(1)} %copy.171), channel_id=1, replica_groups=mesh['acq'=4,'tile'=64] {'acq'}, dimensions={0} | all-to-all | bytes 262144 | tf_op jit(solution)/shard_map/all_to_all | solution.py:121
  391.3 0.7 copy.205
  (56 shorter events, 11.4 us)
Async XLA Ops:
  0.0 61.6 %collective-permute-start.1 = (bf16[4,2,128,1280]{3,2,1,0:T(8,128)(2,1)}, bf16[4,2,128,1280]{3,2,1,0:T(8,128)(2,1)}, u32[]{:S(2)}, u32[]{:S(2)}) collective-permute-start(bf16[4,2,128,1280]{3,2,1,0:T(8,128)(2,1)} %param.6), channel_id=1, source_target_pairs={{0,128},{64,192},{128,0},{192,64},{1,129},{65,193},{129,1},{193,65... | collective-permute-start | bytes 7864328 | tf_op jit(solution)/shard_map/ppermute | solution.py:16
  2.1 114.5 %collective-permute-start = (bf16[4,2,128,1280]{3,2,1,0:T(8,128)(2,1)}, bf16[4,2,128,1280]{3,2,1,0:T(8,128)(2,1)}, u32[]{:S(2)}, u32[]{:S(2)}) collective-permute-start(bf16[4,2,128,1280]{3,2,1,0:T(8,128)(2,1)} %param.6), channel_id=1, source_target_pairs={{0,64},{64,0},{128,192},{192,128},{1,65},{65,1},{129,193},{193,129... | collective-permute-start | bytes 7864328 | tf_op jit(solution)/shard_map/ppermute | solution.py:16
  119.1 1.7 copy-start
  119.1 2.5 copy-start.1
where the time goes:
time: 392 us
  blocking collectives  139 us (35%)
  waiting for transfers between devices  105 us (27%)
  local copies, waits for them, and re-layouts  96 us (24%)
  other arithmetic  34.8 us (9%)
  matrix products  13.3 us (3%)
    psum x1, blocking collectives, shards(): lax.psum(jnp.sum(local_looked[:, 0] ** 2 + local_looked[:, 1] ** 2, axis=...  131 us
    ppermute x2, waiting for transfers between devices, swapped(): lax.ppermute(x, axis, [(i, i ^ 1 << stride) for i in range(lax.axis_size(...  105 us
    another operation x4, local copies, waits for them, and re-layouts, cross_looks(): stacked = jnp.stack([real_part, imag_part], axis=1)  85.9 us
    reduce_sum x2, other arithmetic, cross_looks(): return jnp.sum(stacked, axis=(3, 5)) / (LOOK_L * LOOK_S)  25.5 us
    all_to_all x1, blocking collectives, shards(): lax.all_to_all(outgoing, 'acq', split_axis=0, concat_axis=0, tiled=True)  8.18 us
  transfers between devices with their start and end apart: 2, of which 2 were waited for; matrix products, arithmetic and copies ran while one was open for 2% of the time, Pallas kernels for 0%

commit v1 on v0

--- a/solution.py
+++ b/solution.py
@@ -79,8 +79,11 @@
         group_tiles = swap_tiles(slc, round_number)
         looked_all[round_number] = cross_looks(slc, group_tiles, own_match)
         local_looked = looked_all[round_number]
-        total = lax.psum(
-            jnp.sum(local_looked[:, 0] ** 2 + local_looked[:, 1] ** 2, axis=(1, 2)), "tile"
+        total = jnp.sum(
+            lax.all_gather(
+                jnp.sum(local_looked[:, 0] ** 2 + local_looked[:, 1] ** 2, axis=(1, 2)), "tile"
+            ),
+            axis=0,
         )
         energy = total / grid_count + energy_eps
         looked = looked_all[round_number]

time: 392 us -> 393 us (level)
    psum x1 -> x0, blocking collectives: 131 us -> none  [shards(): lax.psum(jnp.sum(local_looked[:, 0] ** 2 + local_looked[:, 1] ** 2, axis=...]
    unnamed x0 -> x1, blocking collectives: none -> 131 us
where the time goes in v1:
time: 393 us
  blocking collectives  139 us (35%)
  waiting for transfers between devices  103 us (26%)
  local copies, waits for them, and re-layouts  97.9 us (25%)
  other arithmetic  34.9 us (9%)
  matrix products  13.3 us (3%)
    unnamed x1, blocking collectives  131 us
    ppermute x2, waiting for transfers between devices, swapped(): lax.ppermute(x, axis, [(i, i ^ 1 << stride) for i in range(lax.axis_size(...  103 us
    another operation x4, local copies, waits for them, and re-layouts, cross_looks(): stacked = jnp.stack([real_part, imag_part], axis=1)  85.9 us
    reduce_sum x2, other arithmetic, cross_looks(): return jnp.sum(stacked, axis=(3, 5)) / (LOOK_L * LOOK_S)  25.5 us
    all_to_all x1, blocking collectives, shards(): lax.all_to_all(outgoing, 'acq', split_axis=0, concat_axis=0, tiled=True)  8.19 us
  transfers between devices with their start and end apart: 2, of which 2 were waited for; matrix products, arithmetic and copies ran while one was open for 2% of the time, Pallas kernels for 0%

profile of v1, /device:TPU:2, one launch (start us, length us, event | category | flops | bytes accessed | tf_op | source)
XLA Modules:
  0.0 392.5 jit_solution(3377520415127960505)
XLA Ops:
  0.0 2.1 collective-permute-start.1
  2.1 1.4 collective-permute-start
  3.6 0.7 convert_element_type.142
  4.3 0.5 broadcast.377
  4.8 1.3 reduce.5
  6.6 1.3 dynamic-slice.2
  8.6 0.8 fusion.240
  9.7 51.9 %collective-permute-done.1 = bf16[4,2,128,1280]{3,2,1,0:T(8,128)(2,1)} collective-permute-done((bf16[4,2,128,1280]{3,2,1,0:T(8,128)(2,1)}, bf16[4,2,128,1280]{3,2,1,0:T(8,128)(2,1)}, u32[]{:S(2)}, u32[]{:S(2)}) %collective-permute-start.1) | collective-permute-done | bytes 2621472 | tf_op jit(solution)/shard_map/ppermute | solution.py:16
  61.6 2.5 gather_fusion.1
  64.0 1.8 broadcast_select_fusion
  65.9 50.8 %collective-permute-done = bf16[4,2,128,1280]{3,2,1,0:T(8,128)(2,1)} collective-permute-done((bf16[4,2,128,1280]{3,2,1,0:T(8,128)(2,1)}, bf16[4,2,128,1280]{3,2,1,0:T(8,128)(2,1)}, u32[]{:S(2)}, u32[]{:S(2)}) %collective-permute-start) | collective-permute-done | bytes 2621472 | tf_op jit(solution)/shard_map/ppermute | solution.py:16
  116.6 2.5 gather_fusion
  119.4 1.4 copy-done
  120.8 0.8 copy-done.1
  121.6 4.0 %fusion = (f32[4,1,128,1280]{3,2,1,0:T(8,128)}, f32[4,1,128,1280]{3,2,1,0:T(8,128)}, f32[4,1,128,1280]{3,2,1,0:T(8,128)S(1)}, f32[4,1,128,1280]{3,2,1,0:T(8,128)}) fusion(bf16[4,2,128,1280]{3,2,1,0:T(8,128)(2,1)S(1)} %broadcast_select_fusion.1, bf16[4,2,128,1280]{3,2,1,0:T(8,128)(2,1)S(1)} %copy-done.1, bf16[4,2,128,1280]{3,2,1,0:T(8,128)(2,1)S(1)} %copy-done), kind=kLoop, calls=%fused_computation.12 | loop fusion | flops 11796480 | bytes 18350080 | tf_op jit(solution)/shard_map/add | solution.py:49
  125.6 21.7 %stack.39 = f32[4,1,32,4,64,20]{5,4,3,2,0,1:T(8,128)} reshape(f32[4,1,128,1280]{3,2,1,0:T(8,128)} %get-tuple-element.12) | data formatting | bytes 5242880 | tf_op jit(solution)/shard_map/stack | solution.py:51
  147.3 21.7 %stack.40 = f32[4,1,32,4,64,20]{5,4,3,2,0,1:T(8,128)} reshape(f32[4,1,128,1280]{3,2,1,0:T(8,128)} %get-tuple-element.13) | data formatting | bytes 5242880 | tf_op jit(solution)/shard_map/stack | solution.py:51
  168.9 12.7 %maximum_reduce_fusion = f32[4,2,32,64]{3,2,0,1:T(8,128)S(1)} fusion(f32[4,1,32,4,64,20]{5,4,3,2,0,1:T(8,128)} %stack.40, f32[4,1,32,4,64,20]{5,4,3,2,0,1:T(8,128)} %stack.39), kind=kLoop, calls=%fused_computation.2 | loop fusion | flops 2605056 | bytes 5308416 | tf_op jit(solution)/shard_map/reduce_sum | solution.py:55
  185.0 21.7 %stack.45 = f32[4,1,32,4,64,20]{5,4,3,2,0,1:T(8,128)} reshape(f32[4,1,128,1280]{3,2,1,0:T(8,128)} %get-tuple-element.17) | data formatting | bytes 5242880 | tf_op jit(solution)/shard_map/stack | solution.py:51
  206.7 20.9 %stack.46 = f32[4,1,32,4,64,20]{5,4,3,2,0,1:T(8,128)} reshape(f32[4,1,128,1280]{3,2,1,0:T(8,128)S(1)} %get-tuple-element.16) | data formatting | bytes 5242880 | tf_op jit(solution)/shard_map/stack | solution.py:51
  227.6 12.7 %maximum_reduce_fusion.1 = f32[4,2,32,64]{3,2,0,1:T(8,128)S(1)} fusion(f32[4,1,32,4,64,20]{5,4,3,2,0,1:T(8,128)} %stack.46, f32[4,1,32,4,64,20]{5,4,3,2,0,1:T(8,128)} %stack.45), kind=kLoop, calls=%fused_computation.3 | loop fusion | flops 2605056 | bytes 5308416 | tf_op jit(solution)/shard_map/reduce_sum | solution.py:55
  240.9 130.9 %all-reduce.2 = (f32[256]{0:T(256)S(1)}, f32[256]{0:T(256)S(1)}) all-reduce(f32[256]{0:T(256)S(1)} %dynamic-update-slice.1, f32[256]{0:T(256)S(1)} %dynamic-update-slice), channel_id=3, replica_groups=mesh['acq'=4,'tile'=64] {'tile'}, use_global_device_ids=true, to_apply=%add.1 | all-reduce | flops 512 | bytes 4096
  372.0 0.5 fusion.60
  372.5 0.5 fusion.56
  376.4 0.5 fusion.48
  376.9 0.5 fusion.44
  377.4 0.5 fusion.9
  378.3 0.5 fusion.8
  380.3 0.5 fusion.5
  381.3 0.5 fusion.4
  383.7 8.2 %all_to_all.5 = bf16[256,2,128]{2,1,0:T(2,128)(2,1)S(1)} all-to-all(bf16[256,2,128]{2,1,0:T(2,128)(2,1)S(1)} %copy.171), channel_id=1, replica_groups=mesh['acq'=4,'tile'=64] {'acq'}, dimensions={0} | all-to-all | bytes 262144 | tf_op jit(solution)/shard_map/all_to_all | solution.py:124
  391.9 0.7 copy.209
  (66 shorter events, 12.5 us)
Async XLA Ops:
  0.0 61.6 %collective-permute-start.1 = (bf16[4,2,128,1280]{3,2,1,0:T(8,128)(2,1)}, bf16[4,2,128,1280]{3,2,1,0:T(8,128)(2,1)}, u32[]{:S(2)}, u32[]{:S(2)}) collective-permute-start(bf16[4,2,128,1280]{3,2,1,0:T(8,128)(2,1)} %param.6), channel_id=1, source_target_pairs={{0,128},{64,192},{128,0},{192,64},{1,129},{65,193},{129,1},{193,65... | collective-permute-start | bytes 7864328 | tf_op jit(solution)/shard_map/ppermute | solution.py:16
  2.1 114.5 %collective-permute-start = (bf16[4,2,128,1280]{3,2,1,0:T(8,128)(2,1)}, bf16[4,2,128,1280]{3,2,1,0:T(8,128)(2,1)}, u32[]{:S(2)}, u32[]{:S(2)}) collective-permute-start(bf16[4,2,128,1280]{3,2,1,0:T(8,128)(2,1)} %param.6), channel_id=1, source_target_pairs={{0,64},{64,0},{128,192},{192,128},{1,65},{65,1},{129,193},{193,129... | collective-permute-start | bytes 7864328 | tf_op jit(solution)/shard_map/ppermute | solution.py:16
  119.1 1.7 copy-start
  119.1 2.5 copy-start.1
